TPU v7x, 32 devices: a whole 2x2x4 slice. The times are simulated.
32 devices in a mesh: space: 8 (over z, x), dir: 4 (over y, core).
Axes of the slice: x: 2, y: 2, z: 4, core: 2. Of those that a mesh axis runs over, the one named last changes fastest.
Arguments:
- incident: float32 [2, 128, 32768], P(None, 'dir', 'space'), may hold values from -6 to 6
- pair_blocks: bfloat16 [768, 2, 128, 128], P('space'), may hold values from -0.046875 to 0.046875
- pair_local: int32 [768], P('space'), may hold values from 0 to 31, as said below
- pair_partner: int32 [768], P('space'), may hold values from 0 to 255, as said below
- pair_count: int32 [8], P('space'), may hold values from 32 to 64, as said below
- self_blocks: bfloat16 [256, 2, 128, 128], P('space'), may hold values from -0.046875 to 0.046875
- far_in: bfloat16 [256, 2, 32, 128], P('space'), may hold values from -0.5 to 0.5
- far_out: bfloat16 [256, 2, 32, 128], P('space'), may hold values from -0.046875 to 0.046875
- far_rank: int32 [256], P('space'), may hold values from 8 to 32
Outputs:
- solution: float32 [2, 128, 32768], P(None, 'dir', 'space')
- intensity: float32 [32768], P('space')
Inputs may be any that keep to these rules, and one draw needn't show every extreme that they name: `pair_local`: local cluster of a pair, from 0 to 31. For the first 32 slots of each index of space the partner lies on the index just before or just after, within 8 clusters of the shared boundary, and the local cluster lies within 8 clusters of that same boundary; on every index that has a neighbour on a side, some pair names that neighbour's cluster farthest from the boundary within that reach. All other slots pair two different clusters of the same index. Pairs may repeat. `pair_partner`: global cluster number of a pair's partner, as described for pair_local. Slots 32 + pair_count[o] to 95 of index o are empty; some index is full in every draw.
All inputs are finite; a program needn't handle non-finite values.
Results may differ from a plain program's by a relative error of at most 0.003.
Values may be sent and summed in bfloat16 or wider, within the bound.
A program may use at most 128 MiB of HBM per device.

v0:
```python
import functools

import jax
import jax.numpy as jnp
from jax import lax
from jax.experimental import pallas as pl
from jax.experimental.pallas import tpu as pltpu
from jax.sharding import PartitionSpec as P

NDIR = 128
ITERS = 3
REMOTE_DEV = 32
UNROLL = 8
F32 = jnp.float32
BF16 = jnp.bfloat16


def solve_small(matrix, vector):
    order = len(vector)
    rows = [list(line) for line in matrix]
    values = list(vector)
    for col in range(order):
        inverse = 1.0 / rows[col][col]
        for row in range(col + 1, order):
            factor = rows[row][col] * inverse
            for other in range(col + 1, order):
                rows[row][other] = rows[row][other] - factor * rows[col][other]
            values[row] = values[row] - factor * values[col]
    result = [None] * order
    for row in range(order - 1, -1, -1):
        total = values[row]
        for other in range(row + 1, order):
            total = total - rows[row][other] * result[other]
        result[row] = total / rows[row][row]
    return result


def least_squares(hess, beta):
    count = len(hess[0])
    g_real = [[None] * count for _ in range(count)]
    g_imag = [[None] * count for _ in range(count)]
    for first in range(count):
        for second in range(count):
            total_r = 0.0
            total_i = 0.0
            for row in range(min(first, second) + 2):
                ha = hess[row][first]
                hb = hess[row][second]
                total_r = total_r + ha[0] * hb[0] + ha[1] * hb[1]
                total_i = total_i + ha[0] * hb[1] - ha[1] * hb[0]
            g_real[first][second] = total_r
            g_imag[first][second] = total_i
    matrix = []
    for first in range(count):
        matrix.append(
            [g_real[first][b] for b in range(count)] + [-g_imag[first][b] for b in range(count)]
        )
    for first in range(count):
        matrix.append(
            [g_imag[first][b] for b in range(count)] + [g_real[first][b] for b in range(count)]
        )
    vector = [beta * hess[0][a][0] for a in range(count)] + [
        -beta * hess[0][a][1] for a in range(count)
    ]
    found = solve_small(matrix, vector)
    return [(found[a], found[a + count]) for a in range(count)]


def times(left, right):
    return lax.dot_general(left, right, (((1,), (0,)), ((), ())), preferred_element_type=F32)


def times_t(left, right):
    return lax.dot_general(left, right, (((1,), (1,)), ((), ())), preferred_element_type=F32)


def combine(by_real, by_imag):
    half = by_real.shape[0] // 2
    return jnp.concatenate(
        [by_real[:half] - by_imag[half:], by_real[half:] + by_imag[:half]], axis=0
    )


def forward(vec, block):
    panels = block.shape[1]
    both = times_t(vec, block)
    return combine(both[:, :panels], both[:, panels:])


def backward(vec, block):
    panels = block.shape[1]
    return combine(times(vec, block[:panels]), times(vec, block[panels:]))


def loop(first, last, step, carry=None, unroll=UNROLL):
    unroll = min(unroll, last - first)

    def several(number, state):
        for inner in range(unroll):
            state = step(first + number * unroll + inner, state)
        return state

    return lax.fori_loop(0, (last - first) // unroll, several, carry)


def kernel(geom, idx, rank, inc, pairs_hbm, selfs_hbm, fin, fout, out, inten, *scratch):
    n, nd, clusters, rim, dirs, panels, ranks, slots = geom
    near_slots = slots - REMOTE_DEV
    half_slots = near_slots // 2
    (
        pairs, selfs, win, wout, v0, v1, v2, vb, own, rimsum, tr,
        halo0, halo1, halo2, give0, give1, give2, take0, take1, take2,
        small_out, small_in, mom_out, mom_in, pow_out, pow_in,
        load_sem, small_s, small_r, mom_s, mom_r, halo_s, halo_r, give_s, give_r, pow_s, pow_r,
    ) = scratch
    basis = [v0, v1, v2]
    halos, gives, takes = [halo0, halo1, halo2], [give0, give1, give2], [take0, take1, take2]
    me = lax.axis_index("space")
    me_dir = lax.axis_index("dir")

    load_pairs = pltpu.make_async_copy(pairs_hbm, pairs, load_sem.at[0])
    load_selfs = pltpu.make_async_copy(selfs_hbm, selfs, load_sem.at[1])
    load_selfs.start()
    load_pairs.start()

    at_prev = 0
    at_last = at_prev + slots + near_slots
    at_mine = at_last + clusters
    at_part = at_mine + slots
    at_rprev = at_part + slots
    at_rlast = at_rprev + REMOTE_DEV

    barrier = pltpu.get_barrier_semaphore()
    for off in range(1, n):
        pl.semaphore_signal(
            barrier, inc=1, device_id={"space": lax.rem(me + off, n)},
            device_id_type=pl.DeviceIdType.MESH,
        )
    for off in range(1, nd):
        pl.semaphore_signal(
            barrier, inc=1, device_id={"dir": lax.rem(me_dir + off, nd)},
            device_id_type=pl.DeviceIdType.MESH,
        )

    @pl.when(me == 0)
    def _():
        for k in range(ITERS):
            halos[k][0:rim] = jnp.zeros((rim, 2 * dirs, panels), BF16)
            takes[k][0:rim] = jnp.zeros((rim, 2 * dirs, panels), BF16)

    @pl.when(me == n - 1)
    def _():
        for k in range(ITERS):
            halos[k][rim : 2 * rim] = jnp.zeros((rim, 2 * dirs, panels), BF16)
            takes[k][rim : 2 * rim] = jnp.zeros((rim, 2 * dirs, panels), BF16)

    rimsum[0] = jnp.zeros((2 * dirs, panels), F32)
    tr[...] = jnp.zeros(tr.shape, F32)
    lane = lax.broadcasted_iota(jnp.int32, (dirs, panels), 1)
    rank_row = lax.rem(lax.broadcasted_iota(jnp.int32, (2 * ranks, panels), 0), ranks)

    def remote(src, dst, send, recv, axis, target):
        return pltpu.make_async_remote_copy(
            src_ref=src, dst_ref=dst, send_sem=send, recv_sem=recv,
            device_id={axis: target}, device_id_type=pl.DeviceIdType.MESH,
        )

    def small_start(number, parts):
        packed = jnp.zeros((dirs, panels), F32)
        for place, part in enumerate(parts):
            packed = jnp.where(lane == place, jnp.sum(part, axis=1, keepdims=True), packed)
        tr[0:dirs] = packed
        small_out[number] = tr[...].T[0:8]
        copies = []
        for off in range(1, n):
            copy = remote(
                small_out.at[number], small_in.at[number, off - 1],
                small_s.at[number, off - 1], small_r.at[number, off - 1],
                "space", lax.rem(me + off, n),
            )
            copy.start()
            copies.append(copy)
        return copies

    def small_sum(number, parts):
        copies = small_start(number, parts)
        total = small_out[number]
        for off, copy in enumerate(copies):
            copy.wait_recv()
            total = total + small_in[number, off]
        for copy in copies:
            copy.wait_send()
        return [total[q : q + 1] for q in range(8)]

    def columns(rows):
        for place, row in enumerate(rows):
            tr[place : place + 1] = row
        turned = tr[...].T
        return [
            jnp.broadcast_to(turned[0:dirs, q : q + 1], (dirs, panels)) for q in range(len(rows))
        ]

    def norm_step(c, total):
        at = pl.ds(pl.multiple_of(c * panels, panels), panels)
        real, imag = inc[0, :, at], inc[1, :, at]
        return total + real * real + imag * imag

    partial = loop(0, clusters, norm_step, jnp.zeros((dirs, panels), F32))

    def mask_step(c, state):
        keep = (rank_row < rank[c]).astype(F32)
        win[c] = (fin[c].astype(F32) * keep).astype(BF16)
        wout[c] = (fout[c].astype(F32) * keep).astype(BF16)
        return state

    pl.semaphore_wait(barrier, n - 1 + nd - 1)
    beta = jnp.sqrt(small_sum(0, [partial])[0])
    loop(0, clusters, mask_step, 0)

    hess = [[None] * ITERS for _ in range(ITERS + 1)]
    zero_row = jnp.zeros((1, panels), F32)
    for row in range(ITERS + 1):
        for col in range(ITERS):
            hess[row][col] = (zero_row, zero_row)
    inverse_beta = columns([1.0 / beta])[0]
    scales = None
    loaded = False

    for k in range(ITERS):
        here = basis[k]

        def make_step(c, moments):
            if k == 0:
                at = pl.ds(pl.multiple_of(c * panels, panels), panels)
                vec = jnp.concatenate(
                    [inc[0, :, at] * inverse_beta, inc[1, :, at] * inverse_beta], axis=0
                )
            else:
                vec = here[c]
                real, imag = vec[:dirs], vec[dirs:]
                for j in range(k):
                    other = basis[j][c]
                    fr, fi = scales[2 * j], scales[2 * j + 1]
                    real = real - (fr * other[:dirs] - fi * other[dirs:])
                    imag = imag - (fr * other[dirs:] + fi * other[:dirs])
                vec = jnp.concatenate([real * scales[2 * k], imag * scales[2 * k]], axis=0)
            here[c] = vec
            rounded = vec.astype(BF16)
            vb[c] = rounded
            return moments + times_t(rounded, win[c])

        to_prev = remote(
            vb.at[0:rim], halos[k].at[rim : 2 * rim], halo_s.at[k, 0], halo_r.at[k, 1],
            "space", lax.rem(me + n - 1, n),
        )
        to_next = remote(
            vb.at[clusters - rim : clusters], halos[k].at[0:rim], halo_s.at[k, 1],
            halo_r.at[k, 0], "space", lax.rem(me + 1, n),
        )
        moments = jnp.zeros((2 * dirs, 2 * ranks), F32)
        moments = loop(0, rim, make_step, moments)

        @pl.when(me > 0)
        def _():
            to_prev.start()

        moments = loop(clusters - rim, clusters, make_step, moments)

        @pl.when(me < n - 1)
        def _():
            to_next.start()

        moments = loop(rim, clusters - rim, make_step, moments)
        mom_r_part = moments[:dirs, :ranks] - moments[dirs:, ranks:]
        mom_i_part = moments[:dirs, ranks:] + moments[dirs:, :ranks]
        mom_out[k] = jnp.concatenate([mom_r_part, mom_i_part], axis=1)
        mom_copies = []
        for off in range(1, n):
            copy = remote(
                mom_out.at[k], mom_in.at[k, off - 1], mom_s.at[k, off - 1],
                mom_r.at[k, off - 1], "space", lax.rem(me + off, n),
            )
            copy.start()
            mom_copies.append(copy)

        if not loaded:
            load_selfs.wait()
            load_pairs.wait()
            loaded = True

        def self_step(c, state):
            own[c] = forward(vb[c], selfs[c])
            return state

        def near_step(first_slot, first_place):
            def step(m, state):
                slot = first_slot + m
                place = first_place + 2 * m
                block = pairs[slot]
                fwd = forward(vb[idx[at_part + slot]], block)
                bwd = backward(vb[idx[at_mine + slot]], block)
                own[clusters + place] = own[idx[at_prev + place]] + fwd
                own[clusters + place + 1] = own[idx[at_prev + place + 1]] + bwd
                return state
            return step

        def remote_step(slot, state):
            place = 2 * half_slots + slot
            block = pairs[slot]
            bwd = backward(vb[idx[at_mine + slot]], block)
            fwd = forward(halos[k][idx[at_part + slot]], block)
            rimsum[1 + slot] = rimsum[idx[at_rprev + slot]] + bwd
            own[clusters + place] = own[idx[at_prev + place]] + fwd
            return state

        def give_step(t, state):
            gives[k][t] = rimsum[idx[at_rlast + t]].astype(BF16)
            return state

        loop(0, clusters, self_step, 0)
        loop(0, half_slots, near_step(REMOTE_DEV, 0), 0)

        @pl.when(me > 0)
        def _():
            to_next.wait_recv()

        @pl.when(me < n - 1)
        def _():
            to_prev.wait_recv()

        loop(0, REMOTE_DEV, remote_step, 0)
        loop(0, 2 * rim, give_step, 0)
        give_prev = remote(
            gives[k].at[0:rim], takes[k].at[rim : 2 * rim], give_s.at[k, 0], give_r.at[k, 1],
            "space", lax.rem(me + n - 1, n),
        )
        give_next = remote(
            gives[k].at[rim : 2 * rim], takes[k].at[0:rim], give_s.at[k, 1], give_r.at[k, 0],
            "space", lax.rem(me + 1, n),
        )

        @pl.when(me > 0)
        def _():
            give_prev.start()

        @pl.when(me < n - 1)
        def _():
            give_next.start()

        loop(
            0, half_slots,
            near_step(REMOTE_DEV + half_slots, 2 * half_slots + REMOTE_DEV), 0,
        )

        total = mom_out[k]
        for off, copy in enumerate(mom_copies):
            copy.wait_recv()
            total = total + mom_in[k, off]
        for copy in mom_copies:
            copy.wait_send()
        left, right = total[:, :ranks], total[:, ranks:]
        spread = jnp.concatenate(
            [
                jnp.concatenate([left, -right], axis=1),
                jnp.concatenate([right, left], axis=1),
            ],
            axis=0,
        ).astype(BF16)

        @pl.when(me > 0)
        def _():
            to_prev.wait_send()
            give_prev.wait_send()
            give_next.wait_recv()

        @pl.when(me < n - 1)
        def _():
            to_next.wait_send()
            give_next.wait_send()
            give_prev.wait_recv()

        def gather_step(shift):
            def step(c, sums):
                vec = own[idx[at_last + c]] + times(spread, wout[c])
                if shift is not None:
                    vec = vec + takes[k][c - shift].astype(F32)
                if k + 1 < ITERS:
                    basis[k + 1][c] = vec
                real, imag = vec[:dirs], vec[dirs:]
                result = []
                for j in range(k + 1):
                    other = basis[j][c]
                    br, bi = other[:dirs], other[dirs:]
                    result.append(sums[2 * j] + (br * real + bi * imag))
                    result.append(sums[2 * j + 1] + (br * imag - bi * real))
                result.append(sums[2 * k + 2] + (real * real + imag * imag))
                return tuple(result)
            return step

        sums = tuple(jnp.zeros((dirs, panels), F32) for _ in range(2 * k + 3))
        sums = loop(0, rim, gather_step(0), sums, 4)
        sums = loop(rim, clusters - rim, gather_step(None), sums, 4)
        sums = loop(clusters - rim, clusters, gather_step(clusters - 2 * rim), sums, 4)
        rows = small_sum(1 + k, sums)
        square = rows[2 * k + 2]
        rest = square
        for j in range(k + 1):
            rest = rest - (rows[2 * j] * rows[2 * j] + rows[2 * j + 1] * rows[2 * j + 1])
            shift = 1.0 if j == k else 0.0
            hess[j][k] = (rows[2 * j] + shift, rows[2 * j + 1])
        size = jnp.sqrt(jnp.maximum(rest, square * 1e-14))
        hess[k + 1][k] = (size, zero_row)
        if k + 1 < ITERS:
            scales = columns([rows[q] for q in range(2 * k + 2)] + [1.0 / size])

    coeffs = least_squares(hess, beta)
    factors = columns([part for pair in coeffs for part in pair])

    def final_step(c, state):
        real = imag = None
        for k in range(ITERS):
            vec = basis[k][c]
            br, bi = vec[:dirs], vec[dirs:]
            fr, fi = factors[2 * k], factors[2 * k + 1]
            add_r, add_i = fr * br - fi * bi, fr * bi + fi * br
            real = add_r if real is None else real + add_r
            imag = add_i if imag is None else imag + add_i
        at = pl.ds(pl.multiple_of(c * panels, panels), panels)
        out[0, :, at] = real
        out[1, :, at] = imag
        pow_out[pl.ds(c, 1)] = jnp.sum(real * real + imag * imag, axis=0, keepdims=True)
        return state

    loop(0, clusters, final_step, 0)
    copies = []
    for off in range(1, nd):
        copy = remote(
            pow_out, pow_in.at[off - 1], pow_s.at[off - 1], pow_r.at[off - 1],
            "dir", lax.rem(me_dir + off, nd),
        )
        copy.start()
        copies.append(copy)
    total = pow_out[...]
    for off, copy in enumerate(copies):
        copy.wait_recv()
        total = total + pow_in[off]
    inten[...] = total * (1.0 / NDIR)
    for copy in copies:
        copy.wait_send()


def plan(me, clusters, rim, pair_local, pair_partner, pair_count):
    slots = pair_local.shape[0]
    near_slots = slots - REMOTE_DEV
    half = near_slots // 2
    first = me * clusters
    partner = pair_partner - first
    side = jnp.clip(jnp.where(partner < 0, partner + rim, partner - clusters + rim), 0, 2 * rim - 1)
    near = jnp.arange(slots, dtype=jnp.int32) >= REMOTE_DEV
    part = jnp.where(near, jnp.clip(partner, 0, clusters - 1), side)
    live = jnp.arange(near_slots, dtype=jnp.int32) < pair_count[0]
    near_keys = jnp.stack([pair_local[REMOTE_DEV:], part[REMOTE_DEV:]], axis=1)
    near_keys = jnp.where(live[:, None], near_keys, -1)
    keys = jnp.concatenate(
        [near_keys[:half].reshape(-1), pair_local[:REMOTE_DEV], near_keys[half:].reshape(-1)]
    )

    def chain(keys, wanted, base, start_of):
        places = jnp.arange(keys.shape[0], dtype=jnp.int32)
        earlier = (keys[None, :] == keys[:, None]) & (places[None, :] < places[:, None])
        before = jnp.max(jnp.where(earlier, places[None, :] + base, start_of(keys)[:, None]), axis=1)
        goal = jnp.arange(wanted, dtype=jnp.int32)
        hit = keys[None, :] == goal[:, None]
        final = jnp.max(jnp.where(hit, places[None, :] + base, start_of(goal)[:, None]), axis=1)
        return before, final

    before, final = chain(keys, clusters, clusters, lambda key: jnp.maximum(key, 0))
    r_before, r_final = chain(part[:REMOTE_DEV], 2 * rim, 1, jnp.zeros_like)
    return jnp.concatenate([before, final, pair_local, part, r_before, r_final])


def body(
    n, nd,
    incident, pair_blocks, pair_local, pair_partner, pair_count,
    self_blocks, far_in, far_out, far_rank,
):
    clusters, _, panels, _ = self_blocks.shape
    ranks = far_in.shape[2]
    slots = pair_blocks.shape[0]
    dirs = incident.shape[1]
    rim = clusters // 4
    me = lax.axis_index("space")
    table = plan(me, clusters, rim, pair_local, pair_partner, pair_count)
    geom = (n, nd, clusters, rim, dirs, panels, ranks, slots)
    rows = 2 * dirs
    dma = pltpu.SemaphoreType.DMA
    vmem = pl.BlockSpec(memory_space=pltpu.VMEM)
    smem = pl.BlockSpec(memory_space=pltpu.SMEM)
    hbm = pl.BlockSpec(memory_space=pl.ANY)
    solution, intensity = pl.pallas_call(
        functools.partial(kernel, geom),
        out_shape=[
            jax.ShapeDtypeStruct(incident.shape, F32),
            jax.ShapeDtypeStruct((clusters, panels), F32),
        ],
        in_specs=[smem, smem, vmem, hbm, hbm, vmem, vmem],
        out_specs=[vmem, vmem],
        scratch_shapes=[
            pltpu.VMEM((slots, 2 * panels, panels), BF16),
            pltpu.VMEM((clusters, 2 * panels, panels), BF16),
            pltpu.VMEM((clusters, 2 * ranks, panels), BF16),
            pltpu.VMEM((clusters, 2 * ranks, panels), BF16),
        ]
        + [pltpu.VMEM((clusters, rows, panels), F32)] * ITERS
        + [
            pltpu.VMEM((clusters, rows, panels), BF16),
            pltpu.VMEM((clusters + 2 * slots - REMOTE_DEV, rows, panels), F32),
            pltpu.VMEM((REMOTE_DEV + 1, rows, panels), F32),
            pltpu.VMEM((panels, panels), F32),
        ]
        + [pltpu.VMEM((2 * rim, rows, panels), BF16)] * (3 * ITERS)
        + [
            pltpu.VMEM((ITERS + 1, 8, panels), F32),
            pltpu.VMEM((ITERS + 1, n - 1, 8, panels), F32),
            pltpu.VMEM((ITERS, dirs, 2 * ranks), F32),
            pltpu.VMEM((ITERS, n - 1, dirs, 2 * ranks), F32),
            pltpu.VMEM((clusters, panels), F32),
            pltpu.VMEM((nd - 1, clusters, panels), F32),
            dma((2,)),
            dma((ITERS + 1, n - 1)),
            dma((ITERS + 1, n - 1)),
            dma((ITERS, n - 1)),
            dma((ITERS, n - 1)),
            dma((ITERS, 2)),
            dma((ITERS, 2)),
            dma((ITERS, 2)),
            dma((ITERS, 2)),
            dma((nd - 1,)),
            dma((nd - 1,)),
        ],
        compiler_params=pltpu.CompilerParams(
            collective_id=0, has_side_effects=True, vmem_limit_bytes=48 * 1024 * 1024
        ),
    )(
        table,
        far_rank,
        incident,
        pair_blocks.reshape(slots, 2 * panels, panels),
        self_blocks.reshape(clusters, 2 * panels, panels),
        far_in.reshape(clusters, 2 * ranks, panels),
        far_out.reshape(clusters, 2 * ranks, panels),
    )
    return solution, intensity.reshape(clusters * panels)


def solution(mesh):
    return jax.shard_map(
        functools.partial(body, mesh.shape["space"], mesh.shape["dir"]),
        mesh=mesh,
        in_specs=(
            P(None, "dir", "space"),
            P("space", None, None, None),
            P("space"),
            P("space"),
            P("space"),
            P("space", None, None, None),
            P("space", None, None, None),
            P("space", None, None, None),
            P("space"),
        ),
        out_specs=(P(None, "dir", "space"), P("space")),
        check_vma=False,
    )
```

profile of v0, /device:TPU:0, one launch (start us, length us, event | category | flops | bytes accessed | tf_op | source)
XLA Modules:
  0.0 91.4 jit_solution(8218551258286731670)
XLA Ops:
  1.3 0.7 compare_select_fusion.1
  2.0 0.1 select_reduce_fusion.3
  2.1 0.2 select_reduce_fusion.2
  2.3 0.7 slice_bitcast_fusion
  3.0 0.1 fusion.3
  3.1 0.1 copy.15
  3.2 0.1 reshape.71
  3.3 0.1 copy.16
  3.4 0.1 reshape.72
  3.5 0.7 broadcast_maximum_fusion
  4.2 0.2 select_reduce_fusion
  4.4 0.2 select_reduce_fusion.1
  4.6 0.7 concatenate.11.idx
  5.3 0.0 copy-start
  5.3 1.6 %copy-done = bf16[32,2,128,128]{3,2,1,0:T(8,128)(2,1)S(1)} copy-done((bf16[32,2,128,128]{3,2,1,0:T(8,128)(2,1)S(1)}, bf16[32,2,128,128]{3,2,1,0:T(8,128)(2,1)}, u32[]{:S(2)}) %copy-start) | copy-done | bytes 2097176
  6.9 0.0 copy-start.1
  6.9 1.2 %copy-done.1 = f32[2,32,4096]{2,1,0:T(8,128)S(1)} copy-done((f32[2,32,4096]{2,1,0:T(8,128)S(1)}, f32[2,32,4096]{2,1,0:T(8,128)}, u32[]{:S(2)}) %copy-start.1) | copy-done | bytes 1048600
  8.2 0.0 copy-start.2
  8.2 1.0 %copy-done.2 = bf16[32,2,32,128]{3,2,1,0:T(8,128)(2,1)S(1)} copy-done((bf16[32,2,32,128]{3,2,1,0:T(8,128)(2,1)S(1)}, bf16[32,2,32,128]{3,2,1,0:T(8,128)(2,1)}, u32[]{:S(2)}) %copy-start.2) | copy-done | bytes 524312
  9.2 1.0 %copy-done.3 = bf16[32,2,32,128]{3,2,1,0:T(8,128)(2,1)S(1)} copy-done((bf16[32,2,32,128]{3,2,1,0:T(8,128)(2,1)S(1)}, bf16[32,2,32,128]{3,2,1,0:T(8,128)(2,1)}, u32[]{:S(2)}) %copy-start.3) | copy-done | bytes 524312
  10.2 0.7 copy-done.4
  10.9 78.9 %shard_map.104 = (f32[2,32,4096]{2,1,0:T(8,128)S(1)}, f32[32,128]{1,0:T(8,128)S(1)}) custom-call(s32[432]{0:T(512)S(1)} %concatenate.11.idx, s32[32]{0:T(128)S(1)} %copy-done.4, f32[2,32,4096]{2,1,0:T(8,128)S(1)} %copy-done.1, bf16[96,256,128]{2,1,0:T(8,128)(2,1)} %bitcast.17, bf16[32,256,128]{2,1,0:T(8,128)(2,1)S(1)} %bitcast.13, ...), custom_call_target="tpu_custom_call" | custom-call | tf_op jit(solution)/shard_map/pallas_call | solution.py:500
  89.8 1.0 %copy.20 = f32[2,32,4096]{2,1,0:T(8,128)} copy(f32[2,32,4096]{2,1,0:T(8,128)S(1)} %get-tuple-element.14) | data formatting | bytes 2097152
  90.8 0.6 copy.21
  (7 shorter events, 0.0 us)
Async XLA Ops:
  5.3 1.6 %copy-start = (bf16[32,2,128,128]{3,2,1,0:T(8,128)(2,1)S(1)}, bf16[32,2,128,128]{3,2,1,0:T(8,128)(2,1)}, u32[]{:S(2)}) copy-start(bf16[32,2,128,128]{3,2,1,0:T(8,128)(2,1)} %param.14) | copy-start | bytes 6291460
  6.9 1.2 %copy-start.1 = (f32[2,32,4096]{2,1,0:T(8,128)S(1)}, f32[2,32,4096]{2,1,0:T(8,128)}, u32[]{:S(2)}) copy-start(f32[2,32,4096]{2,1,0:T(8,128)} %inc.1) | copy-start | bytes 3145732
  8.2 1.0 %copy-start.2 = (bf16[32,2,32,128]{3,2,1,0:T(8,128)(2,1)S(1)}, bf16[32,2,32,128]{3,2,1,0:T(8,128)(2,1)}, u32[]{:S(2)}) copy-start(bf16[32,2,32,128]{3,2,1,0:T(8,128)(2,1)} %param.15) | copy-start | bytes 1572868
  9.2 1.0 %copy-start.3 = (bf16[32,2,32,128]{3,2,1,0:T(8,128)(2,1)S(1)}, bf16[32,2,32,128]{3,2,1,0:T(8,128)(2,1)}, u32[]{:S(2)}) copy-start(bf16[32,2,32,128]{3,2,1,0:T(8,128)(2,1)} %param.16) | copy-start | bytes 1572868
  10.2 0.7 copy-start.4
where the time goes:
time: 91.7 us; the launch traced here: 91.4 us
  Pallas kernels  78.9 us (86%)
  local copies, waits for them, and re-layouts  9.06 us (10%)
  other arithmetic  2.1 us (2%)
  between operations  1.33 us (1%)
    pallas_call x1, Pallas kernels, body(): pl.pallas_call(functools.partial(kernel, geom), out_shape=[jax.ShapeDtype...  78.9 us
    unnamed x12, local copies, waits for them, and re-layouts  7.13 us

commit v1 on v0

--- a/solution.py
+++ b/solution.py
@@ -10,7 +10,7 @@
 NDIR = 128
 ITERS = 3
 REMOTE_DEV = 32
-UNROLL = 8
+UNROLL = 16
 F32 = jnp.float32
 BF16 = jnp.bfloat16
 
@@ -103,12 +103,15 @@
     return lax.fori_loop(0, (last - first) // unroll, several, carry)
 
 
-def kernel(geom, idx, rank, inc, pairs_hbm, selfs_hbm, fin, fout, out, inten, *scratch):
+def kernel(
+    geom, local, partner, count, rank, inc_hbm, pairs_hbm, selfs_hbm, fin_hbm, fout_hbm,
+    out, inten, *scratch,
+):
     n, nd, clusters, rim, dirs, panels, ranks, slots = geom
     near_slots = slots - REMOTE_DEV
     half_slots = near_slots // 2
     (
-        pairs, selfs, win, wout, v0, v1, v2, vb, own, rimsum, tr,
+        inc, pairs, selfs, win, wout, table, idx, v0, v1, v2, vb, own, rimsum, tr,
         halo0, halo1, halo2, give0, give1, give2, take0, take1, take2,
         small_out, small_in, mom_out, mom_in, pow_out, pow_in,
         load_sem, small_s, small_r, mom_s, mom_r, halo_s, halo_r, give_s, give_r, pow_s, pow_r,
@@ -118,17 +121,19 @@
     me = lax.axis_index("space")
     me_dir = lax.axis_index("dir")
 
-    load_pairs = pltpu.make_async_copy(pairs_hbm, pairs, load_sem.at[0])
-    load_selfs = pltpu.make_async_copy(selfs_hbm, selfs, load_sem.at[1])
-    load_selfs.start()
-    load_pairs.start()
-
-    at_prev = 0
-    at_last = at_prev + slots + near_slots
-    at_mine = at_last + clusters
-    at_part = at_mine + slots
-    at_rprev = at_part + slots
-    at_rlast = at_rprev + REMOTE_DEV
+    loads = [
+        pltpu.make_async_copy(src, dst, load_sem.at[number])
+        for number, (src, dst) in enumerate(
+            [
+                (inc_hbm, inc), (fin_hbm, win), (fout_hbm, wout), (selfs_hbm, selfs),
+                (pairs_hbm, pairs),
+            ]
+        )
+    ]
+    for load in loads:
+        load.start()
+    load_inc, load_in, load_out, load_selfs, load_pairs = loads
+    load_table = pltpu.make_async_copy(table, idx, load_sem.at[len(loads)])
 
     barrier = pltpu.get_barrier_semaphore()
     for off in range(1, n):
@@ -182,8 +187,7 @@
             copies.append(copy)
         return copies
 
-    def small_sum(number, parts):
-        copies = small_start(number, parts)
+    def small_finish(number, copies):
         total = small_out[number]
         for off, copy in enumerate(copies):
             copy.wait_recv()
@@ -200,22 +204,95 @@
             jnp.broadcast_to(turned[0:dirs, q : q + 1], (dirs, panels)) for q in range(len(rows))
         ]
 
+    def make_table():
+        spot = lax.broadcasted_iota(jnp.int32, (1, panels), 1)
+        order = jnp.where(
+            spot < REMOTE_DEV, spot + half_slots,
+            jnp.where(spot < REMOTE_DEV + half_slots, spot - REMOTE_DEV, spot),
+        )
+        base = me * clusters
+
+        def near_part(slot):
+            return jnp.clip(partner[slot] - base, 0, clusters - 1)
+
+        def side_part(slot):
+            offset = partner[slot] - base
+            return jnp.clip(
+                jnp.where(offset < 0, offset + rim, offset - clusters + rim), 0, 2 * rim - 1
+            )
+
+        def key_step(part_of):
+            def step(slot, keys):
+                first, second = keys
+                here = spot == slot
+                return (
+                    jnp.where(here, local[slot], first), jnp.where(here, part_of(slot), second)
+                )
+            return step
+
+        none = jnp.full((1, panels), -1, jnp.int32)
+        keys = loop(0, REMOTE_DEV, key_step(side_part), (none, none))
+        key_i, parts = loop(REMOTE_DEV, slots, key_step(near_part), keys)
+        live = (spot < REMOTE_DEV) | (spot - REMOTE_DEV < count[0])
+        key_i = jnp.where(live, key_i, -1)
+        key_j = jnp.where(live & (spot >= REMOTE_DEV), parts, -1)
+        key_r = jnp.where(spot < REMOTE_DEV, parts, -1)
+
+        def put(state, key, when, entry):
+            prev_i, prev_j, last = state
+            prev_i = jnp.where((key_i == key) & (2 * order > when), entry, prev_i)
+            prev_j = jnp.where((key_j == key) & (2 * order + 1 > when), entry, prev_j)
+            return prev_i, prev_j, jnp.where(spot == key, entry, last)
+
+        def near_put(shift):
+            def step(slot, state):
+                alive = slot - REMOTE_DEV < count[0]
+                when = 2 * (slot - shift)
+                state = put(state, jnp.where(alive, local[slot], -2), when, clusters + slot)
+                return put(
+                    state, jnp.where(alive, near_part(slot), -2), when + 1, clusters + slots + slot
+                )
+            return step
+
+        def remote_put(slot, state):
+            chain, prev_r, last_r = state
+            chain = put(chain, local[slot], 2 * (slot + half_slots), clusters + slot)
+            key = side_part(slot)
+            prev_r = jnp.where((key_r == key) & (spot > slot), 1 + slot, prev_r)
+            return chain, prev_r, jnp.where(spot == key, 1 + slot, last_r)
+
+        zeros = jnp.zeros((1, panels), jnp.int32)
+        chain = (jnp.maximum(key_i, 0), jnp.maximum(key_j, 0), spot)
+        chain = loop(REMOTE_DEV, REMOTE_DEV + half_slots, near_put(REMOTE_DEV), chain)
+        chain, prev_r, last_r = loop(0, REMOTE_DEV, remote_put, (chain, zeros, zeros))
+        chain = loop(REMOTE_DEV + half_slots, slots, near_put(0), chain)
+        rows = [chain[0], chain[1], chain[2], parts, prev_r, last_r]
+        for place, row in enumerate(rows):
+            table[place : place + 1] = row
+
     def norm_step(c, total):
         at = pl.ds(pl.multiple_of(c * panels, panels), panels)
         real, imag = inc[0, :, at], inc[1, :, at]
         return total + real * real + imag * imag
 
+    load_inc.wait()
     partial = loop(0, clusters, norm_step, jnp.zeros((dirs, panels), F32))
 
     def mask_step(c, state):
         keep = (rank_row < rank[c]).astype(F32)
-        win[c] = (fin[c].astype(F32) * keep).astype(BF16)
-        wout[c] = (fout[c].astype(F32) * keep).astype(BF16)
+        win[c] = (win[c].astype(F32) * keep).astype(BF16)
+        wout[c] = (wout[c].astype(F32) * keep).astype(BF16)
         return state
 
     pl.semaphore_wait(barrier, n - 1 + nd - 1)
-    beta = jnp.sqrt(small_sum(0, [partial])[0])
+    flying = small_start(0, [partial])
+    make_table()
+    load_table.start()
+    load_in.wait()
+    load_out.wait()
     loop(0, clusters, mask_step, 0)
+    load_table.wait()
+    beta = jnp.sqrt(small_finish(0, flying)[0])
 
     hess = [[None] * ITERS for _ in range(ITERS + 1)]
     zero_row = jnp.zeros((1, panels), F32)
@@ -292,33 +369,31 @@
             own[c] = forward(vb[c], selfs[c])
             return state
 
-        def near_step(first_slot, first_place):
+        def near_step(first_slot):
             def step(m, state):
                 slot = first_slot + m
-                place = first_place + 2 * m
                 block = pairs[slot]
-                fwd = forward(vb[idx[at_part + slot]], block)
-                bwd = backward(vb[idx[at_mine + slot]], block)
-                own[clusters + place] = own[idx[at_prev + place]] + fwd
-                own[clusters + place + 1] = own[idx[at_prev + place + 1]] + bwd
+                fwd = forward(vb[idx[3, slot]], block)
+                bwd = backward(vb[local[slot]], block)
+                own[clusters + slot] = own[idx[0, slot]] + fwd
+                own[clusters + slots + slot] = own[idx[1, slot]] + bwd
                 return state
             return step
 
         def remote_step(slot, state):
-            place = 2 * half_slots + slot
             block = pairs[slot]
-            bwd = backward(vb[idx[at_mine + slot]], block)
-            fwd = forward(halos[k][idx[at_part + slot]], block)
-            rimsum[1 + slot] = rimsum[idx[at_rprev + slot]] + bwd
-            own[clusters + place] = own[idx[at_prev + place]] + fwd
+            bwd = backward(vb[local[slot]], block)
+            fwd = forward(halos[k][idx[3, slot]], block)
+            rimsum[1 + slot] = rimsum[idx[4, slot]] + bwd
+            own[clusters + slot] = own[idx[0, slot]] + fwd
             return state
 
         def give_step(t, state):
-            gives[k][t] = rimsum[idx[at_rlast + t]].astype(BF16)
+            gives[k][t] = rimsum[idx[5, t]].astype(BF16)
             return state
 
         loop(0, clusters, self_step, 0)
-        loop(0, half_slots, near_step(REMOTE_DEV, 0), 0)
+        loop(0, half_slots, near_step(REMOTE_DEV), 0)
 
         @pl.when(me > 0)
         def _():
@@ -349,7 +424,7 @@
 
         loop(
             0, half_slots,
-            near_step(REMOTE_DEV + half_slots, 2 * half_slots + REMOTE_DEV), 0,
+            near_step(REMOTE_DEV + half_slots), 0,
         )
 
         total = mom_out[k]
@@ -381,7 +456,7 @@
 
         def gather_step(shift):
             def step(c, sums):
-                vec = own[idx[at_last + c]] + times(spread, wout[c])
+                vec = own[idx[2, c]] + times(spread, wout[c])
                 if shift is not None:
                     vec = vec + takes[k][c - shift].astype(F32)
                 if k + 1 < ITERS:
@@ -401,7 +476,7 @@
         sums = loop(0, rim, gather_step(0), sums, 4)
         sums = loop(rim, clusters - rim, gather_step(None), sums, 4)
         sums = loop(clusters - rim, clusters, gather_step(clusters - 2 * rim), sums, 4)
-        rows = small_sum(1 + k, sums)
+        rows = small_finish(1 + k, small_start(1 + k, sums))
         square = rows[2 * k + 2]
         rest = square
         for j in range(k + 1):
@@ -449,36 +524,6 @@
         copy.wait_send()
 
 
-def plan(me, clusters, rim, pair_local, pair_partner, pair_count):
-    slots = pair_local.shape[0]
-    near_slots = slots - REMOTE_DEV
-    half = near_slots // 2
-    first = me * clusters
-    partner = pair_partner - first
-    side = jnp.clip(jnp.where(partner < 0, partner + rim, partner - clusters + rim), 0, 2 * rim - 1)
-    near = jnp.arange(slots, dtype=jnp.int32) >= REMOTE_DEV
-    part = jnp.where(near, jnp.clip(partner, 0, clusters - 1), side)
-    live = jnp.arange(near_slots, dtype=jnp.int32) < pair_count[0]
-    near_keys = jnp.stack([pair_local[REMOTE_DEV:], part[REMOTE_DEV:]], axis=1)
-    near_keys = jnp.where(live[:, None], near_keys, -1)
-    keys = jnp.concatenate(
-        [near_keys[:half].reshape(-1), pair_local[:REMOTE_DEV], near_keys[half:].reshape(-1)]
-    )
-
-    def chain(keys, wanted, base, start_of):
-        places = jnp.arange(keys.shape[0], dtype=jnp.int32)
-        earlier = (keys[None, :] == keys[:, None]) & (places[None, :] < places[:, None])
-        before = jnp.max(jnp.where(earlier, places[None, :] + base, start_of(keys)[:, None]), axis=1)
-        goal = jnp.arange(wanted, dtype=jnp.int32)
-        hit = keys[None, :] == goal[:, None]
-        final = jnp.max(jnp.where(hit, places[None, :] + base, start_of(goal)[:, None]), axis=1)
-        return before, final
-
-    before, final = chain(keys, clusters, clusters, lambda key: jnp.maximum(key, 0))
-    r_before, r_final = chain(part[:REMOTE_DEV], 2 * rim, 1, jnp.zeros_like)
-    return jnp.concatenate([before, final, pair_local, part, r_before, r_final])
-
-
 def body(
     n, nd,
     incident, pair_blocks, pair_local, pair_partner, pair_count,
@@ -489,8 +534,6 @@
     slots = pair_blocks.shape[0]
     dirs = incident.shape[1]
     rim = clusters // 4
-    me = lax.axis_index("space")
-    table = plan(me, clusters, rim, pair_local, pair_partner, pair_count)
     geom = (n, nd, clusters, rim, dirs, panels, ranks, slots)
     rows = 2 * dirs
     dma = pltpu.SemaphoreType.DMA
@@ -503,18 +546,21 @@
             jax.ShapeDtypeStruct(incident.shape, F32),
             jax.ShapeDtypeStruct((clusters, panels), F32),
         ],
-        in_specs=[smem, smem, vmem, hbm, hbm, vmem, vmem],
+        in_specs=[smem] * 4 + [hbm] * 5,
         out_specs=[vmem, vmem],
         scratch_shapes=[
+            pltpu.VMEM(incident.shape, F32),
             pltpu.VMEM((slots, 2 * panels, panels), BF16),
             pltpu.VMEM((clusters, 2 * panels, panels), BF16),
             pltpu.VMEM((clusters, 2 * ranks, panels), BF16),
             pltpu.VMEM((clusters, 2 * ranks, panels), BF16),
+            pltpu.VMEM((8, panels), jnp.int32),
+            pltpu.SMEM((8, panels), jnp.int32),
         ]
         + [pltpu.VMEM((clusters, rows, panels), F32)] * ITERS
         + [
             pltpu.VMEM((clusters, rows, panels), BF16),
-            pltpu.VMEM((clusters + 2 * slots - REMOTE_DEV, rows, panels), F32),
+            pltpu.VMEM((clusters + 2 * slots, rows, panels), F32),
             pltpu.VMEM((REMOTE_DEV + 1, rows, panels), F32),
             pltpu.VMEM((panels, panels), F32),
         ]
@@ -526,7 +572,7 @@
             pltpu.VMEM((ITERS, n - 1, dirs, 2 * ranks), F32),
             pltpu.VMEM((clusters, panels), F32),
             pltpu.VMEM((nd - 1, clusters, panels), F32),
-            dma((2,)),
+            dma((6,)),
             dma((ITERS + 1, n - 1)),
             dma((ITERS + 1, n - 1)),
             dma((ITERS, n - 1)),
@@ -539,10 +585,12 @@
             dma((nd - 1,)),
         ],
         compiler_params=pltpu.CompilerParams(
-            collective_id=0, has_side_effects=True, vmem_limit_bytes=48 * 1024 * 1024
+            collective_id=0, has_side_effects=True, vmem_limit_bytes=60 * 1024 * 1024
         ),
     )(
-        table,
+        pair_local,
+        pair_partner,
+        pair_count,
         far_rank,
         incident,
         pair_blocks.reshape(slots, 2 * panels, panels),

time: 91.7 us -> 85.3 us (0.930)
  local copies, waits for them, and re-layouts: 9.06 us -> 3.59 us
  other arithmetic: 2.1 us -> 0 us
  Pallas kernels: 78.9 us -> 80.1 us
    unnamed x12 -> x2, local copies, waits for them, and re-layouts: 7.13 us -> 3.59 us
    pallas_call x1, Pallas kernels: 78.9 us -> 80.1 us  [body(): pl.pallas_call(functools.partial(kernel, geom), out_shape=[jax.ShapeDtype...]
where the time goes in v1:
time: 85.3 us; the launch traced here: 85 us
  Pallas kernels  80.1 us (94%)
  local copies, waits for them, and re-layouts  3.59 us (4%)
  between operations  1.29 us (2%)
    pallas_call x1, Pallas kernels, body(): pl.pallas_call(functools.partial(kernel, geom), out_shape=[jax.ShapeDtype...  80.1 us
    unnamed x2, local copies, waits for them, and re-layouts  3.59 us

profile of v1, /device:TPU:0, one launch (start us, length us, event | category | flops | bytes accessed | tf_op | source)
XLA Modules:
  0.0 85.0 jit_solution(12372971629539485171)
XLA Ops:
  1.3 80.1 %shard_map.104 = (f32[2,32,4096]{2,1,0:T(8,128)}, f32[32,128]{1,0:T(8,128)}) custom-call(s32[96]{0:T(128)} %local.1, s32[96]{0:T(128)} %partner.1, s32[1]{0:T(128)S(6)} %copy.13.count, s32[32]{0:T(128)} %rank.1, f32[2,32,4096]{2,1,0:T(8,128)} %inc_hbm.1, bf16[96,256,128]{2,1,0:T(8,128)(2,1)} %bitcast.5, bf16[32,256,128]{2,1,0:T(8,128)(2,1)} %bitcast.6, ...), custom_call_target="tpu_custom_call" | custom-call | tf_op jit(solution)/shard_map/pallas_call | solution.py:543
  81.4 2.3 %copy.14 = f32[2,32,4096]{2,1,0:T(8,128)} copy(f32[2,32,4096]{2,1,0:T(8,128)} %get-tuple-element.8) | data formatting | bytes 2097152
  83.7 1.3 %copy.15 = f32[4096]{0:T(1024)} copy(f32[4096]{0:T(1024)} %bitcast.9) | data formatting | bytes 32768
